TPU v7x, 512 devices: a whole 4x4x16 slice. The times are simulated.
512 devices in a mesh: grow: 16 (over x, y), gcol: 32 (over z, core).
Axes of the slice: x: 4, y: 4, z: 16, core: 2. Of those that a mesh axis runs over, the one named last changes fastest.
Arguments:
- pair_matrix: bfloat16 [3, 2, 16384, 512], P(None, None, 'grow', 'gcol'), may hold values from -2 to 2
- valence_index: int32 [3, 512], replicated, may hold values from 0 to 2047
- conduction_index: int32 [3, 512], replicated, may hold values from 0 to 2047
- valence_energy: float32 [2048], replicated, may hold values from -12 to 0
- conduction_energy: float32 [2048], replicated, may hold values from 0.5 to 20
Outputs:
- chi: float32 [2, 16384, 16384], P(None, 'grow', 'gcol')
All inputs are finite; a program needn't handle non-finite values.
Results may differ from a plain program's by a relative error of at most 0.0028.
Values may be sent and summed in bfloat16 or wider, within the bound.
A program may use at most 64 MiB of HBM per device.

v0:
```python
import jax
import jax.numpy as jnp
from jax import lax
from jax.sharding import PartitionSpec as P


def spread(value, axis, source):
    kept = jnp.where(lax.axis_index(axis) == source, value, 0).astype(value.dtype)
    return lax.psum(kept, axis)


def weigh_block(block, scale):
    blk_real = (block[..., 0, :, :].astype(jnp.float32) * scale).astype(jnp.bfloat16)
    blk_imag = (-block[..., 1, :, :].astype(jnp.float32) * scale).astype(jnp.bfloat16)
    return jnp.stack([blk_real, blk_imag], axis=-3)


def outer_terms(rows, block):
    real_part = jnp.einsum(
        "rp,cp->rc", rows[0], block[0], preferred_element_type=jnp.float32
    ) - jnp.einsum("rp,cp->rc", rows[1], block[1], preferred_element_type=jnp.float32)
    imag_part = jnp.einsum(
        "rp,cp->rc", rows[0], block[1], preferred_element_type=jnp.float32
    ) + jnp.einsum("rp,cp->rc", rows[1], block[0], preferred_element_type=jnp.float32)
    return jnp.stack([real_part, imag_part])


def shards(pair_matrix, valence_index, conduction_index, valence_energy, conduction_energy):
    factor = lax.axis_size("gcol") // lax.axis_size("grow")
    column = lax.axis_index("gcol")
    root_row = column // factor
    half_index = column % factor
    weight = 2.0 / (
        jnp.take(valence_energy, valence_index) - jnp.take(conduction_energy, conduction_index)
    )
    panels = pair_matrix.shape[0]
    row_count = pair_matrix.shape[2]
    col_count = row_count // factor
    gathered = jnp.stack(
        [lax.all_gather(pair_matrix[panel], "gcol", axis=2, tiled=True) for panel in range(panels)]
    )
    own_half = lax.dynamic_slice_in_dim(gathered, half_index * col_count, col_count, 2)
    blocks = spread(weigh_block(own_half, weight[:, None, :]), "grow", root_row)
    total = jnp.zeros((2, row_count, col_count), jnp.float32)
    for panel in range(panels):
        total = total + outer_terms(gathered[panel], blocks[panel])
    return total


def solution(mesh):
    in_specs = (P(None, None, "grow", "gcol"), P(), P(), P(), P())
    out_specs = P(None, "grow", "gcol")
    return jax.shard_map(shards, mesh=mesh, in_specs=in_specs, out_specs=out_specs, check_vma=False)
```

profile of v0, /device:TPU:1, one launch (start us, length us, event | category | flops | bytes accessed | tf_op | source)
XLA Modules:
  0.0 382.8 jit_solution(16508669201424896139)
XLA Ops:
  6.5 0.0 copy-start
  6.5 0.0 all-gather.11.cloned.1.call-start
  6.5 1.6 fusion.10
  8.1 0.0 all-gather.11.cloned.1.call-update
  8.1 0.0 all-gather.7.cloned.1.call-start
  8.2 0.7 all-gather.7.cloned.1.call-update
  8.9 0.0 all-gather.9.cloned.1.call-start
  8.9 0.7 all-gather.9.cloned.1.call-update
  9.6 0.0 all-reduce.2.cloned.1.call-start
  9.7 0.7 compare_select_fusion.1
  10.4 0.0 copy-done
  10.4 0.0 copy-start.6
  10.4 8.4 %gather_fusion = f32[1536]{0:T(1024)S(1)} fusion(f32[2048]{0:T(1024)S(1)} %copy-done, s32[2048]{0:T(1024)S(1)} %pad_clamp_fusion.1), kind=kCustom, calls=%fused_computation.clone | custom fusion | bytes 18432 | tf_op jit(solution)/shard_map/jit(_take)/gather | solution.py:34
  18.8 0.0 copy-start.1
  18.9 0.0 copy-done.6
  18.9 0.6 copy-done.1
  19.5 0.0 copy-start.7
  19.5 8.4 %gather_fusion.1 = f32[1536]{0:T(1024)S(1)} fusion(f32[2048]{0:T(1024)S(1)} %copy-done.1, s32[2048]{0:T(1024)S(1)} %pad_clamp_fusion), kind=kCustom, calls=%fused_computation.1.clone | custom fusion | bytes 18432 | tf_op jit(solution)/shard_map/jit(_take)/gather | solution.py:34
  28.0 0.0 copy-done.7
  28.0 59.1 %all-gather.11.cloned.1.call-done = bf16[1,2,1024,512]{2,3,1,0:T(8,128)(2,1)} async-done(((bf16[1,2,1024,16]{2,3,1,0:T(8,128)(2,1)}), bf16[1,2,1024,512]{2,3,1,0:T(8,128)(2,1)}) %all-gather.11.cloned.1.call-update) | async-done | bytes 2097168 | tf_op jit(solution)/shard_map/all_gather | solution.py:40
  87.1 70.9 %all-gather.7.cloned.1.call-done = bf16[1,2,1024,512]{2,3,1,0:T(8,128)(2,1)} async-done(((bf16[1,2,1024,16]{2,3,1,0:T(8,128)(2,1)}), bf16[1,2,1024,512]{2,3,1,0:T(8,128)(2,1)}) %all-gather.7.cloned.1.call-update) | async-done | bytes 2097168 | tf_op jit(solution)/shard_map/all_gather | solution.py:40
  158.1 71.0 %all-gather.9.cloned.1.call-done = bf16[1,2,1024,512]{2,3,1,0:T(8,128)(2,1)} async-done(((bf16[1,2,1024,16]{2,3,1,0:T(8,128)(2,1)}), bf16[1,2,1024,512]{2,3,1,0:T(8,128)(2,1)}) %all-gather.9.cloned.1.call-update) | async-done | bytes 2097168 | tf_op jit(solution)/shard_map/all_gather | solution.py:40
  229.0 2.2 fusion.2
  231.3 0.7 multiply_convert_fusion.1
  232.0 2.0 maximum_select_fusion
  234.0 0.0 copy-start.2
  234.0 0.0 all-reduce.2.cloned.1.call-update
  234.0 122.8 %all-reduce.2.cloned.1.call-done = bf16[3,2,512,512]{2,3,1,0:T(8,128)(2,1)} async-done(((bf16[3,2,512,512]{2,3,1,0:T(8,128)(2,1)}), bf16[3,2,512,512]{2,3,1,0:T(8,128)(2,1)}) %all-reduce.2.cloned.1.call-update) | async-done | bytes 3145744 | tf_op jit(solution)/shard_map/psum | solution.py:9
  356.8 0.0 copy-done.2
  356.8 0.0 copy-start.4
  356.8 0.0 copy-start.5
  356.8 1.9 fusion.7
  358.7 0.0 copy-done.4
  358.7 0.0 copy-start.3
  358.7 1.9 fusion.5
  360.6 0.0 copy-done.5
  360.6 0.0 copy-done.3
  360.7 0.7 fusion.3
  361.4 0.7 fusion.8
  362.1 0.7 fusion.6
  362.9 0.7 fusion.4
  363.6 0.8 add_bitcast_fusion
  364.4 0.7 add_bitcast_fusion.1
  365.1 0.7 add_bitcast_fusion.2
  365.8 0.8 subtract_bitcast_fusion
  366.6 0.7 subtract_bitcast_fusion.1
  367.3 0.7 subtract_bitcast_fusion.2
  368.1 2.8 fusion
  370.9 5.4 %copy.7 = f32[2,1024,512]{2,1,0:T(8,128)} copy(f32[2,1024,512]{1,2,0:T(8,128)} %fusion) | data formatting | bytes 8388608 | tf_op jit(solution)/shard_map/add | solution.py:46
  (8 shorter events, 0.1 us)
Async XLA Ops:
  6.5 3.9 %copy-start = (f32[2048]{0:T(1024)S(1)}, f32[2048]{0:T(1024)}, u32[]{:S(2)}) copy-start(f32[2048]{0:T(1024)} %param.10) | copy-start | bytes 24580
  6.5 80.6 %all-gather.11.cloned.1.call-start = ((), (), s32[]{:S(2)}) async-start(), calls=%async_computation.3 | async-start | bytes 2162688 | tf_op jit(solution)/shard_map/all_gather | solution.py:40
  8.1 149.9 %all-gather.7.cloned.1.call-start = ((), (), s32[]{:S(2)}) async-start(), calls=%async_computation.1 | async-start | bytes 2162688 | tf_op jit(solution)/shard_map/all_gather | solution.py:40
  8.9 220.2 %all-gather.9.cloned.1.call-start = ((), (), s32[]{:S(2)}) async-start(), calls=%async_computation.2 | async-start | bytes 2162688 | tf_op jit(solution)/shard_map/all_gather | solution.py:40
  9.6 347.1 %all-reduce.2.cloned.1.call-start = ((), (), s32[]{:S(2)}) async-start(), calls=%async_computation | async-start | bytes 6291456 | tf_op jit(solution)/shard_map/psum | solution.py:9
  10.4 8.4 %copy-start.6 = (s32[3,512]{1,0:T(4,128)S(1)}, s32[3,512]{1,0:T(4,128)}, u32[]{:S(2)}) copy-start(s32[3,512]{1,0:T(4,128)} %param.9) | copy-start | bytes 18436
  18.8 0.7 copy-start.1
  19.5 8.4 %copy-start.7 = (s32[3,512]{1,0:T(4,128)S(1)}, s32[3,512]{1,0:T(4,128)}, u32[]{:S(2)}) copy-start(s32[3,512]{1,0:T(4,128)} %param.8) | copy-start | bytes 18436
  234.0 122.8 %copy-start.2 = (bf16[1,2,1024,512]{2,3,1,0:T(8,128)(2,1)S(1)}, bf16[1,2,1024,512]{2,3,1,0:T(8,128)(2,1)}, u32[]{:S(2)}) copy-start(bf16[1,2,1024,512]{2,3,1,0:T(8,128)(2,1)} %all-gather.11.cloned.1.call-done) | copy-start | bytes 6291460
  356.8 1.9 copy-start.4
  356.8 3.9 %copy-start.5 = (bf16[3,2,512,512]{2,3,1,0:T(8,128)(2,1)S(1)}, bf16[3,2,512,512]{2,3,1,0:T(8,128)(2,1)}, u32[]{:S(2)}) copy-start(bf16[3,2,512,512]{2,3,1,0:T(8,128)(2,1)} %all-reduce.2.cloned.1.call-done) | copy-start | bytes 9437188
  358.7 2.0 copy-start.3
Sparse Core Ops, SparseCore 0:
  9.5 77.5 all-gather.10
  89.3 68.7 all-gather.6
  160.2 68.7 all-gather.8
  234.1 122.5 all-reduce.1
where the time goes:
time: 383 us
  waiting for transfers between devices  325 us (85%)
  local copies, waits for them, and re-layouts  24.4 us (6%)
  between operations  13.4 us (3%)
  matrix products  11.2 us (3%)
  other arithmetic  8.44 us (2%)
    all_gather x3, waiting for transfers between devices, shards(): lax.all_gather(pair_matrix[panel], 'gcol', axis=2, tiled=True)  201 us
    psum x1, waiting for transfers between devices, spread(): return lax.psum(kept, axis)  123 us
    gather x2, local copies, waits for them, and re-layouts, shards(): jnp.take(valence_energy, valence_index)  8.4 us
    gather x2, local copies, waits for them, and re-layouts, shards(): jnp.take(conduction_energy, conduction_index)  8.39 us
  transfers between devices with their start and end apart: 4, of which 4 were waited for; matrix products, arithmetic and copies ran while one was open for 5% of the time, Pallas kernels for 0%

commit v1 on v0

v1 whole, which is shorter than its diff:
```python
import functools

import jax
import jax.numpy as jnp
from jax import lax
from jax.experimental import pallas as pl
from jax.experimental.pallas import tpu as pltpu
from jax.sharding import PartitionSpec as P

MESH = pl.DeviceIdType.MESH
SIDE = 4
DEEP = 16
SUB = 32
LAST = 26
HOP = 2
ROWS = 256

TREE = {
    (1, 0): (1, 0), (3, 0): (3, 0), (2, 0): (1, 0), (1, 2): (0, 2), (3, 1): (0, 1), (3, 3): (0, 3),
    (1, 1): (0, 3), (1, 3): (0, 1), (2, 3): (0, 3), (3, 2): (0, 1), (2, 1): (3, 0), (0, 3): (1, 0),
    (0, 1): (1, 0), (0, 2): (3, 0), (2, 2): (1, 0),
}
STEPS = [(1, 0), (3, 0), (0, 1), (0, 3), (0, 2), (2, 0)]


def node_depth(node):
    depth = 0
    while node != (0, 0):
        step = TREE[node]
        node = ((node[0] - step[0]) % SIDE, (node[1] - step[1]) % SIDE)
        depth += 1
    return depth


def tree_tables():
    masks, depths, slots = {}, 0, {}
    count = [0] * (SIDE * SIDE)
    for step in STEPS:
        for node, used in sorted(TREE.items()):
            if used == step:
                parent = ((node[0] - step[0]) % SIDE, (node[1] - step[1]) % SIDE)
                place = parent[0] * SIDE + parent[1]
                slots.setdefault(step, [0] * (SIDE * SIDE))[place] = count[place]
                masks[step] = masks.get(step, 0) | (1 << place)
                count[place] += 1
    for node in TREE:
        depths |= node_depth(node) << (2 * (node[0] * SIDE + node[1]))
    lanes = {s: sum(v << (2 * p) for p, v in enumerate(slots[s])) for s in slots}
    signed = lambda v: v - (1 << 32) if v >= (1 << 31) else v
    return masks, signed(depths), {s: signed(v) for s, v in lanes.items()}, max(count)


MASKS, DEPTHS, LANES, MOST = tree_tables()


def turn(step, times):
    for _ in range(times):
        step = ((-step[1]) % SIDE, step[0] % SIDE)
    return step


def slot_of(s, way, core):
    return jnp.where(s == 0, core, 4 * s - 2 + jnp.where(s == 8, 0, 2 * way) + core)


def far_part(way, sub, core):
    return (sub == 2 * way) | ((sub == 1) & (core == way))


def kernel(x_ref, vi_ref, ci_ref, ve_ref, ce_ref, out_ref, rows_buf, cols_buf, rhs, acc, wcol, ibuf,
           zsend, zrecv, dsend, drecv, csend, crecv, osem):
    g = lax.axis_index("grow")
    gc = lax.axis_index("gcol")
    x, y, z, c = g // SIDE, g % SIDE, gc // 2, gc % 2
    dx, dy = (x - z // SIDE + SIDE) % SIDE, (y - z % SIDE + SIDE) % SIDE
    is_root = (dx == 0) & (dy == 0)

    def plane(step, core):
        return {"grow": ((x + step[0]) % SIDE) * SIDE + (y + step[1]) % SIDE, "gcol": z * 2 + core}

    def along(way):
        return {"grow": g, "gcol": ((z + (1 if way == 0 else DEEP - 1)) % DEEP) * 2 + c}

    sibling = {"grow": g, "gcol": z * 2 + 1 - c}

    barrier = pltpu.get_barrier_semaphore()
    others = [along(0), along(1), sibling] + [plane(s, k) for s in STEPS for k in range(2)]
    for other in others:
        pl.semaphore_signal(barrier, inc=1, device_id=other, device_id_type=MESH)
    rows_buf[c] = x_ref[...]
    pl.semaphore_wait(barrier, len(others))

    def piece(i):
        return i // 3, i % 3

    def zcopy(way, i):
        s, sub = piece(i)
        at = pl.ds(pl.multiple_of(sub * SUB, SUB), SUB)
        return pltpu.make_async_remote_copy(
            src_ref=rows_buf.at[slot_of(s, way, c), at],
            dst_ref=rows_buf.at[slot_of(s + 1, way, c), at],
            send_sem=zsend.at[way, i], recv_sem=zrecv.at[way, i + 3],
            device_id=along(way), device_id_type=MESH)

    def zsends(way, i):
        s, sub = piece(i)
        return (s < 7) | ((s == 7) & far_part(way, sub, c))

    def dcopy(slot):
        return pltpu.make_async_remote_copy(
            src_ref=rows_buf.at[slot], dst_ref=rows_buf.at[slot],
            send_sem=dsend.at[slot], recv_sem=drecv.at[slot],
            device_id=sibling, device_id_type=MESH)

    def cvalid(way, core, i):
        s, sub = piece(i)
        return ((s == 0) & (way == 0)) | ((s > 0) & (s < 8)) | ((s == 8) & far_part(way, sub, core))

    def root_copies(way, core, i):
        s, sub = piece(i)
        slot = slot_of(s, way, core)
        at = pl.ds(pl.multiple_of(sub * SUB, SUB), SUB)
        tree = 2 * way + core
        copies = []
        for n, step in enumerate(s for s in STEPS if MASKS.get(s, 0) & 1):
            for half in range(2):
                copies.append(pltpu.make_async_remote_copy(
                    src_ref=rows_buf.at[slot, at, half * 512:(half + 1) * 512],
                    dst_ref=cols_buf.at[slot, at],
                    send_sem=csend.at[tree, i, 2 * n + half], recv_sem=crecv.at[tree, i],
                    device_id=plane(turn(step, tree), half), device_id_type=MESH))
        return copies

    def place_in(tree):
        px, py = dx, dy
        for _ in range(tree):
            px, py = py, (SIDE - px) % SIDE
        return px * SIDE + py

    places = [place_in(t) for t in range(4)]
    lags = [HOP * ((DEPTHS >> (2 * places[t])) & 3) for t in range(4)]

    def ccopy(tree, i, step):
        s, sub = piece(i)
        slot = slot_of(s, tree // 2, tree % 2)
        at = pl.ds(pl.multiple_of(sub * SUB, SUB), SUB)
        lane = (LANES[step] >> (2 * places[tree])) & 3
        return pltpu.make_async_remote_copy(
            src_ref=cols_buf.at[slot, at], dst_ref=cols_buf.at[slot, at],
            send_sem=csend.at[tree, i, lane], recv_sem=crecv.at[tree, i],
            device_id=plane(turn(step, tree), c), device_id_type=MESH)

    def passes(tree, step):
        return ((MASKS[step] >> places[tree]) & 1) == 1

    def z_turn(i):
        s, sub = piece(i)
        for way in range(2):
            have = ((s > 0) & (s < 8)) | ((s == 8) & far_part(way, sub, c))

            @pl.when(have)
            def _():
                zcopy(way, i - 3).wait_recv()

            @pl.when(zsends(way, i))
            def _():
                zcopy(way, i).start()

            for core in range(2):
                @pl.when(is_root & (c == core) & cvalid(way, core, i))
                def _():
                    for copy in root_copies(way, core, i):
                        copy.start()

            @pl.when((sub == 2) & (s > 0) & (s < 8))
            def _():
                dcopy(slot_of(s, way, c)).start()

        @pl.when(i == LAST)
        def _():
            dcopy(30 + c).start()

    def c_turn(i):
        for tree in range(4):
            j = i - lags[tree]

            @pl.when((j >= 0) & (j <= LAST) & cvalid(tree // 2, tree % 2, j))
            def _():
                ccopy(tree, j, STEPS[0]).wait_recv()
                for step in STEPS:
                    if step in MASKS:
                        @pl.when(passes(tree, step))
                        def _():
                            ccopy(tree, j, step).start()

    def drain(i):
        for way in range(2):
            @pl.when(zsends(way, i))
            def _():
                zcopy(way, i).wait_send()

            for core in range(2):
                @pl.when(is_root & (c == core) & cvalid(way, core, i))
                def _():
                    for copy in root_copies(way, core, i):
                        copy.wait_send()
        for tree in range(4):
            @pl.when(jnp.logical_not(is_root) & cvalid(tree // 2, tree % 2, i))
            def _():
                for step in STEPS:
                    if step in MASKS:
                        @pl.when(passes(tree, step))
                        def _():
                            ccopy(tree, i, step).wait_send()

    def weights():
        def look(table, index):
            out = []
            for j in range(4):
                at = index[:, j * 128:(j + 1) * 128]
                low, high = at & 127, at >> 7
                value = jnp.zeros((8, 128), jnp.float32)
                for r in range(16):
                    row = jnp.broadcast_to(table[r:r + 1, :], (8, 128))
                    value = jnp.where(high == r, jnp.take_along_axis(row, low, axis=1), value)
                out.append(value)
            return out

        ibuf[...] = jnp.zeros_like(ibuf)
        ibuf[0, 0:3, :] = vi_ref[...]
        ibuf[1, 0:3, :] = ci_ref[...]
        low = look(ve_ref, ibuf[0])
        high = look(ce_ref, ibuf[1])
        for j in range(4):
            w = 2.0 / (low[j] - high[j])
            for k in range(3):
                wcol[k, j * 128:(j + 1) * 128, :] = jnp.broadcast_to(w[k:k + 1, :], (128, 128)).T

    def build(first, count):
        def arrived(q):
            @pl.when(q % 2 != c)
            def _():
                dcopy(q).wait_recv()

        def fill(load):
            @pl.loop(0, count)
            def _(n):
                q = first + n
                s, way, core = (q + 2) // 4, ((q + 2) % 4) // 2, q % 2
                chip = (z + jnp.where(way == 1, s, DEEP - s)) % DEEP
                band = pl.multiple_of((2 * chip + core) * 16, 16)
                base = n * 96
                for k in range(3):
                    w = wcol[k, pl.ds(band, 16), :]
                    w = jnp.concatenate([w] * 4, axis=1)
                    re = (load(q, 32 * k).astype(jnp.float32) * w).astype(jnp.bfloat16)
                    im = (load(q, 32 * k + 16).astype(jnp.float32) * w).astype(jnp.bfloat16)
                    top = pl.ds(pl.multiple_of(base + 32 * k, 16), 16)
                    low = pl.ds(pl.multiple_of(base + 32 * k + 16, 16), 16)
                    rhs[top, 0:512] = re
                    rhs[low, 0:512] = im
                    rhs[top, 512:1024] = -im
                    rhs[low, 512:1024] = re

        @pl.loop(0, count)
        def _(n):
            arrived(first + n)

        @pl.when(is_root)
        def _():
            half = pl.ds(pl.multiple_of(c * 512, 512), 512)
            fill(lambda q, r: rows_buf[q, r:r + 16, half])

        @pl.when(jnp.logical_not(is_root))
        def _():
            fill(lambda q, r: cols_buf[q, r:r + 16, :])

    def block(first, count, r, fresh):
        at = pl.ds(pl.multiple_of(r * ROWS, ROWS), ROWS)
        left = rows_buf[first:first + count, :, at].reshape(count * 96, ROWS)
        value = lax.dot_general(left, rhs[0:count * 96, :], (((0,), (0,)), ((), ())),
                                preferred_element_type=jnp.float32)
        if fresh:
            acc[at, :] = value
        else:
            acc[at, :] += value

    def write(r):
        at = pl.ds(pl.multiple_of(r * ROWS, ROWS), ROWS)
        return [pltpu.make_async_copy(acc.at[at, part * 512:(part + 1) * 512], out_ref.at[part, at], osem.at[part, r])
                for part in range(2)]

    blocks = 1024 // ROWS
    groups = [(0, 6), (6, 8), (14, 8), (22, 8), (30, 2)]
    slack = 3 * HOP
    ready = [3 * s + 2 + slack for s in (1, 3, 5, 7)]

    z_turn(jnp.int32(0))
    z_turn(jnp.int32(1))
    z_turn(jnp.int32(2))
    dcopy(c).start()
    weights()

    @pl.loop(0, LAST + slack + 1)
    def _(i):
        @pl.when((i > 2) & (i <= LAST))
        def _():
            z_turn(i)

        @pl.when(jnp.logical_not(is_root))
        def _():
            c_turn(i)

        for n, begin in enumerate(ready):
            first, count = groups[n]

            @pl.when(i == begin)
            def _():
                build(first, count)

            @pl.when((i >= begin) & (i < begin + blocks))
            def _():
                block(first, count, i - begin, n == 0)

        @pl.when(i >= slack + 3)
        def _():
            drain(i - slack - 3)

    build(*groups[4])

    @pl.loop(0, blocks)
    def _(r):
        block(groups[4][0], groups[4][1], r, False)
        for copy in write(r):
            copy.start()

    @pl.loop(LAST - 2, LAST + 1)
    def _(i):
        drain(i)

    @pl.loop(0, 32)
    def _(q):
        @pl.when(q % 2 == c)
        def _():
            dcopy(q).wait_send()

    @pl.loop(0, blocks)
    def _(r):
        for copy in write(r):
            copy.wait()


def shards(pair_matrix, valence_index, conduction_index, valence_energy, conduction_energy):
    x = jnp.swapaxes(pair_matrix, 2, 3).reshape(96, 1024)
    vmem = pl.BlockSpec(memory_space=pltpu.VMEM)
    return pl.pallas_call(
        kernel,
        out_shape=jax.ShapeDtypeStruct((2, 1024, 512), jnp.float32),
        in_specs=[vmem] * 5,
        out_specs=pl.BlockSpec(memory_space=pl.ANY),
        scratch_shapes=[
            pltpu.VMEM((32, 96, 1024), jnp.bfloat16),
            pltpu.VMEM((32, 96, 512), jnp.bfloat16),
            pltpu.VMEM((768, 1024), jnp.bfloat16),
            pltpu.VMEM((1024, 1024), jnp.float32),
            pltpu.VMEM((3, 512, 128), jnp.float32),
            pltpu.VMEM((2, 8, 512), jnp.int32),
            pltpu.SemaphoreType.DMA((2, LAST + 1)),
            pltpu.SemaphoreType.DMA((2, LAST + 1)),
            pltpu.SemaphoreType.DMA((32,)),
            pltpu.SemaphoreType.DMA((32,)),
            pltpu.SemaphoreType.DMA((4, LAST + 1, 4)),
            pltpu.SemaphoreType.DMA((4, LAST + 1)),
            pltpu.SemaphoreType.DMA((2, 1024 // ROWS)),
        ],
        compiler_params=pltpu.CompilerParams(collective_id=0, has_side_effects=True, vmem_limit_bytes=40 << 20),
        cost_estimate=pl.CostEstimate(flops=6 << 30, bytes_accessed=4 << 20, transcendentals=0),
        name="chi",
    )(x, valence_index, conduction_index, valence_energy.reshape(16, 128), conduction_energy.reshape(16, 128))


def solution(mesh):
    in_specs = (P(None, None, "grow", "gcol"), P(), P(), P(), P())
    out_specs = P(None, "grow", "gcol")
    return jax.shard_map(shards, mesh=mesh, in_specs=in_specs, out_specs=out_specs, check_vma=False)
```

time: 383 us -> 82.5 us (0.22)
  the two profiles are of different devices: /device:TPU:1 before, /device:TPU:4 now
where the time goes in v1:
time: 82.5 us; the launch traced here: 82.1 us
  Pallas kernels  76.4 us (93%)
  local copies, waits for them, and re-layouts  5.73 us (7%)
    pallas_call x1, Pallas kernels, shards(): pl.pallas_call(kernel, out_shape=jax.ShapeDtypeStruct((2, 1024, 512), jnp...  76.4 us
    unnamed x11, local copies, waits for them, and re-layouts  5.73 us

profile of v1, /device:TPU:4, one launch (start us, length us, event | category | flops | bytes accessed | tf_op | source)
XLA Modules:
  0.0 82.1 jit_solution(3811446007618974789)
XLA Ops:
  0.0 0.0 copy-start
  0.0 0.9 %copy-done = bf16[3,2,1024,16]{2,3,1,0:T(8,128)(2,1)S(1)} copy-done((bf16[3,2,1024,16]{2,3,1,0:T(8,128)(2,1)S(1)}, bf16[3,2,1024,16]{2,3,1,0:T(8,128)(2,1)}, u32[]{:S(2)}) %copy-start) | copy-done | bytes 196632
  0.9 0.0 copy-start.1
  0.9 0.7 copy-done.1
  1.6 0.0 copy-start.2
  1.6 0.7 copy-done.2
  2.3 0.0 copy-start.3
  2.3 0.7 copy-done.3
  3.0 0.0 copy-start.4
  3.0 0.7 copy-done.4
  3.7 76.4 %chi.1 = f32[2,1024,512]{2,1,0:T(8,128)S(1)} custom-call(bf16[96,1024]{1,0:T(8,128)(2,1)S(1)} %bitcast.5, s32[3,512]{1,0:T(4,128)S(1)} %copy-done.1, s32[3,512]{1,0:T(4,128)S(1)} %copy-done.2, f32[16,128]{1,0:T(8,128)S(1)} %bitcast.6, f32[16,128]{1,0:T(8,128)S(1)} %bitcast.7), custom_call_target="tpu_custom_call" | custom-call | flops 6442450944 | bytes 4194304 | tf_op jit(solution)/shard_map/chi/pallas_call | solution.py:356
  80.1 2.0 %copy.7 = f32[2,1024,512]{2,1,0:T(8,128)} copy(f32[2,1024,512]{2,1,0:T(8,128)S(1)} %chi.1) | data formatting | bytes 8388608
Async XLA Ops:
  0.0 0.9 %copy-start = (bf16[3,2,1024,16]{2,3,1,0:T(8,128)(2,1)S(1)}, bf16[3,2,1024,16]{2,3,1,0:T(8,128)(2,1)}, u32[]{:S(2)}) copy-start(bf16[3,2,1024,16]{2,3,1,0:T(8,128)(2,1)} %param.5) | copy-start | bytes 589828
  0.9 0.7 copy-start.1
  1.6 0.7 copy-start.2
  2.3 0.7 copy-start.3
  3.0 0.7 copy-start.4

commit v2 on v0

v2 whole, which is shorter than its diff:
```python
import functools

import jax
import jax.numpy as jnp
from jax import lax
from jax.experimental import pallas as pl
from jax.experimental.pallas import tpu as pltpu
from jax.sharding import PartitionSpec as P

MESH = pl.DeviceIdType.MESH
SIDE = 4
DEEP = 16
SUB = 32
LAST = 26
HOP = 2
ROWS = 512

TREES = [
    {
        (1, 0): (0, 1), (1, 3): (1, 0), (2, 3): (0, 3), (2, 1): (0, 3), (0, 1): (0, 3), (1, 2): (0, 3),
        (0, 3): (0, 3), (3, 3): (3, 0), (3, 0): (0, 1), (2, 2): (3, 0), (3, 2): (0, 3), (1, 1): (0, 3),
        (0, 2): (3, 0), (2, 0): (3, 0), (3, 1): (0, 3),
    },
    {
        (1, 0): (1, 0), (3, 0): (3, 0), (2, 0): (1, 0), (1, 2): (0, 2), (3, 1): (0, 1), (3, 3): (0, 3),
        (1, 1): (0, 3), (1, 3): (0, 1), (2, 3): (0, 3), (3, 2): (0, 1), (2, 1): (3, 0), (0, 3): (1, 0),
        (0, 1): (1, 0), (0, 2): (3, 0), (2, 2): (1, 0),
    },
]
SPLIT = 20
STEPS = [(1, 0), (3, 0), (0, 1), (0, 3), (0, 2), (2, 0)]


def children_of(tree, node):
    return [s for s in STEPS if tree.get(((node[0] + s[0]) % SIDE, (node[1] + s[1]) % SIDE)) == s]


def node_depth(tree, node):
    depth = 0
    while node != (0, 0):
        step = tree[node]
        node = ((node[0] - step[0]) % SIDE, (node[1] - step[1]) % SIDE)
        depth += 1
    return depth


NODES = [(px, py) for px in range(SIDE) for py in range(SIDE)]
ROOT_FANS = [children_of(t, (0, 0)) for t in TREES]
FAN = max(len(children_of(t, n)) for t in TREES for n in NODES if n != (0, 0))
DEEPEST = [max(node_depth(t, n) for n in NODES) for t in TREES]


def pick(place, values):
    shift = max(max(values).bit_length(), 1)
    per = 31 // shift
    result = jnp.int32(0)
    for start in range(0, len(values), per):
        part = values[start:start + per]
        word = sum(v << (shift * n) for n, v in enumerate(part))
        if word:
            here = (place >= start) & (place < start + per)
            offset = jnp.where(here, place - start, 0) * shift
            result = result + jnp.where(here, (word >> offset) & ((1 << shift) - 1), 0)
    return result


def turn(step, times):
    for _ in range(times):
        step = ((-step[1]) % SIDE, step[0] % SIDE)
    return step


def piece(i):
    s = (i * 11) >> 5
    return s, i - 3 * s


def slot_of(s, way, core):
    if way == 0:
        return jnp.where(s == 0, core, 4 * s - 2 + core)
    return jnp.where(s == 0, core, jnp.where(s == 8, 30 + core, 4 * s + core))


def far_part(way, sub, core):
    return (sub == 2 * way) | ((sub == 1) & (core == way))


def kernel(x_hbm, vi_hbm, ci_hbm, ve_hbm, ce_hbm, out_ref, rows_buf, cols_buf, rhs, wcol, vi_ref, ci_ref, ve_ref, ce_ref, ibuf,
           isem, zsend, zrecv, dsend, drecv, csend, crecv):
    g = lax.axis_index("grow")
    gc = lax.axis_index("gcol")
    x, y, z, c = g // SIDE, g % SIDE, gc // 2, gc % 2
    dx, dy = (x - z // SIDE + SIDE) % SIDE, (y - z % SIDE + SIDE) % SIDE
    is_root = (dx == 0) & (dy == 0)

    parts = [(x_hbm.at[SUB * k:SUB * (k + 1), 512 * h:512 * (h + 1)], rows_buf.at[3 * c + k, h])
             for k in range(3) for h in range(2)]
    parts += [(vi_hbm, vi_ref), (ci_hbm, ci_ref), (ve_hbm, ve_ref), (ce_hbm, ce_ref)]
    loads = [pltpu.make_async_copy(src, dst, isem.at[max(n - 5, 0)]) for n, (src, dst) in enumerate(parts)]
    for load in loads:
        load.start()

    def grow_at(step):
        return ((x + step[0]) % SIDE) * SIDE + (y + step[1]) % SIDE

    def dev(grow, gcol):
        return {"grow": grow, "gcol": gcol}

    ends = [((z + 1) % DEEP) * 2 + c, ((z + DEEP - 1) % DEEP) * 2 + c]
    sibling = dev(g, z * 2 + 1 - c)

    barrier = pltpu.get_barrier_semaphore()
    others = [dev(g, ends[0]), dev(g, ends[1]), sibling]
    others += [dev(grow_at(s), z * 2 + k) for s in STEPS for k in range(2)]
    for other in others:
        pl.semaphore_signal(barrier, inc=1, device_id=other, device_id_type=MESH)

    depths, fans, kids = [[], []], [[], []], [[], []]

    def find_roles():
        px, py = dx, dy
        for tree in range(4):
            place = px * SIDE + py
            for kind, table in enumerate(TREES):
                depths[kind].append(pick(place, [node_depth(table, n) for n in NODES]))
                lists = [children_of(table, n) if n != (0, 0) else [] for n in NODES]
                fans[kind].append(pick(place, [len(v) for v in lists]))
                mine = []
                for n in range(FAN):
                    codes = [STEPS.index(v[n]) if n < len(v) else 0 for v in lists]
                    code = pick(place, codes)
                    chip = jnp.int32(0)
                    for k in sorted(set(codes)):
                        chip = jnp.where(code == k, grow_at(turn(STEPS[k], tree)), chip)
                    mine.append(chip)
                kids[kind].append(mine)
            px, py = py, (SIDE - px) % SIDE

    def arrival(ref, sem):
        pltpu.make_async_copy(ref, ref, sem).wait()

    def zcopy(way, i):
        s, sub = piece(i)
        return pltpu.make_async_remote_copy(
            src_ref=rows_buf.at[3 * slot_of(s, way, c) + sub],
            dst_ref=rows_buf.at[3 * slot_of(s + 1, way, c) + sub],
            send_sem=zsend.at[0], recv_sem=zrecv.at[way, i],
            device_id=dev(g, ends[way]), device_id_type=MESH)

    def dcopy(slot):
        return pltpu.make_async_remote_copy(
            src_ref=rows_buf.at[pl.ds(3 * slot, 3)], dst_ref=rows_buf.at[pl.ds(3 * slot, 3)],
            send_sem=dsend.at[0], recv_sem=drecv.at[(slot + 2) >> 3],
            device_id=sibling, device_id_type=MESH)

    def root_copies(kind, way, i):
        s, sub = piece(i)
        slot = slot_of(s, way, c)
        tree = 2 * way + c
        copies = []
        for n, step in enumerate(ROOT_FANS[kind]):
            chip = jnp.where(c == 0, grow_at(turn(step, 2 * way)), grow_at(turn(step, 2 * way + 1)))
            for half in range(2):
                copies.append(pltpu.make_async_remote_copy(
                    src_ref=rows_buf.at[3 * slot + sub, half],
                    dst_ref=cols_buf.at[3 * slot + sub],
                    send_sem=csend.at[kind, tree, 2 * n + half], recv_sem=crecv.at[tree, i],
                    device_id=dev(chip, z * 2 + half), device_id_type=MESH))
        return copies

    def ccopy(kind, tree, i, n):
        s, sub = piece(i)
        slot = slot_of(s, tree // 2, tree % 2)
        return pltpu.make_async_remote_copy(
            src_ref=cols_buf.at[3 * slot + sub], dst_ref=cols_buf.at[3 * slot + sub],
            send_sem=csend.at[kind, tree, n], recv_sem=crecv.at[tree, i],
            device_id=dev(kids[kind][tree][n], gc), device_id_type=MESH)

    def z_turn(i, own=False):
        s, sub = piece(i)
        far = [far_part(way, sub, c) for way in range(2)]
        for way in range(2):
            if not own:
                @pl.when((s < 8) | far[way])
                def _():
                    zcopy(way, i - 3).wait_recv()

            @pl.when((s < 7) | ((s == 7) & far[way]))
            def _():
                zcopy(way, i).start()

        @pl.when(is_root)
        def _():
            for kind in range(2):
                @pl.when((i <= SPLIT) if kind == 0 else (i > SPLIT))
                def _():
                    for way in range(1 if own else 2):
                        if kind == 0:
                            for copy in root_copies(kind, way, i):
                                copy.start()
                        else:
                            @pl.when((s < 8) | far[way])
                            def _():
                                for copy in root_copies(kind, way, i):
                                    copy.start()

        if not own:
            @pl.when(sub == 2)
            def _():
                dcopy(slot_of(s, 0, c)).start()

                @pl.when(s < 8)
                def _():
                    dcopy(slot_of(s, 1, c)).start()

    def c_turn(kind, i):
        for tree in range(4):
            j = i - HOP * depths[kind][tree]
            if kind == 0:
                ok = (j >= 3 * (tree // 2)) & (j <= SPLIT)
            else:
                s, sub = piece(j)
                ok = (j > SPLIT) & ((s < 8) | ((j <= LAST) & far_part(tree // 2, sub, tree % 2)))

            @pl.when(ok)
            def _():
                ccopy(kind, tree, j, 0).wait_recv()

                def pass_on(n):
                    @pl.when(fans[kind][tree] > n)
                    def _():
                        ccopy(kind, tree, j, n).start()
                        if n + 1 < FAN:
                            pass_on(n + 1)

                pass_on(0)

    def drain(kind):
        def sent(tree, n, more):
            count = SPLIT + 1 - 3 * more if kind == 0 else 23 - SPLIT + more
            arrival(cols_buf.at[0:count], csend.at[kind, tree, n])

        @pl.when(is_root)
        def _():
            for way in range(2):
                for core in range(2):
                    @pl.when(c == core)
                    def _():
                        for n in range(2 * len(ROOT_FANS[kind])):
                            sent(2 * way + core, n, way if kind == 0 else 1 + (way == core))

        @pl.when(jnp.logical_not(is_root))
        def _():
            for tree in range(4):
                way, core = tree // 2, tree % 2
                for n in range(FAN):
                    @pl.when(fans[kind][tree] > n)
                    def _():
                        sent(tree, n, way if kind == 0 else 1 + (way == core))

    def drain_rows():
        arrival(rows_buf.at[0:45], zsend.at[0])
        arrival(rows_buf.at[0:48], dsend.at[0])

    def weights(j):
        lanes = pl.ds(pl.multiple_of(j * 128, 128), 128)

        def look(table, index):
            low, high = index & 127, index >> 7
            value = jnp.zeros((8, 128), jnp.float32)
            for r in range(16):
                row = jnp.broadcast_to(table[r:r + 1, :], (8, 128))
                value = jnp.where(high == r, jnp.take_along_axis(row, low, axis=1), value)
            return value

        @pl.when(j == 0)
        def _():
            for load in loads[6:]:
                load.wait()
            ibuf[...] = jnp.zeros_like(ibuf)
            ibuf[0, 0:3, :] = vi_ref[...]
            ibuf[1, 0:3, :] = ci_ref[...]

        w = 2.0 / (look(ve_ref, ibuf[0, :, lanes]) - look(ce_ref, ibuf[1, :, lanes]))
        for k in range(3):
            wcol[k, lanes, :] = jnp.broadcast_to(w[k:k + 1, :], (128, 128)).T

    def build(first, count):
        def fill(load):
            @pl.loop(0, count)
            def _(n):
                q = first + n
                s, way, core = (q + 2) // 4, ((q + 2) % 4) // 2, q % 2
                chip = (z + jnp.where(way == 1, s, DEEP - s)) % DEEP
                band = pl.multiple_of((2 * chip + core) * 16, 16)
                base = n * 96
                for k in range(3):
                    w = wcol[k, pl.ds(band, 16), :]
                    w = jnp.concatenate([w] * 4, axis=1)
                    re = (load(q, k, 0).astype(jnp.float32) * w).astype(jnp.bfloat16)
                    im = (load(q, k, 16).astype(jnp.float32) * w).astype(jnp.bfloat16)
                    top = pl.ds(pl.multiple_of(base + 32 * k, 16), 16)
                    low = pl.ds(pl.multiple_of(base + 32 * k + 16, 16), 16)
                    rhs[top, 0:512] = re
                    rhs[low, 0:512] = im
                    rhs[top, 512:1024] = -im
                    rhs[low, 512:1024] = re

        arrival(rows_buf.at[0:3 * count // 2], drecv.at[(first + 2) >> 3])

        @pl.when(is_root)
        def _():
            fill(lambda q, k, r: rows_buf[3 * q + k, c, r:r + 16, :])

        @pl.when(jnp.logical_not(is_root))
        def _():
            fill(lambda q, k, r: cols_buf[3 * q + k, r:r + 16, :])

    def block(first, count, r, fresh):
        at = pl.ds(pl.multiple_of(r * ROWS, ROWS), ROWS)
        left = rows_buf[3 * first:3 * (first + count), r].reshape(count * 96, ROWS)
        value = lax.dot_general(left, rhs[0:count * 96, :], (((0,), (0,)), ((), ())),
                                preferred_element_type=jnp.float32)
        for part in range(2):
            if fresh:
                out_ref[part, at, :] = value[:, part * 512:(part + 1) * 512]
            else:
                out_ref[part, at, :] += value[:, part * 512:(part + 1) * 512]

    blocks = 1024 // ROWS
    groups = [(0, 6), (6, 8), (14, 8), (22, 8), (30, 2)]
    depth0, depth1 = HOP * DEEPEST[0], HOP * DEEPEST[1]

    def ready(last_s):
        i = 3 * last_s + 2
        return i + depth0 if i <= SPLIT else max(SPLIT + depth0, i + depth1)

    begins = [ready(s) for s in (1, 3, 5, 7)]
    turns = LAST + depth1 + 1

    find_roles()
    arrival(rows_buf.at[pl.ds(3 * c, 3)], isem.at[0])
    pl.semaphore_wait(barrier, len(others))
    for i in range(3):
        z_turn(jnp.int32(i), own=True)
    dcopy(c).start()

    @pl.loop(0, turns)
    def _(i):
        @pl.when((i > 2) & (i <= LAST))
        def _():
            z_turn(i)

        @pl.when(jnp.logical_not(is_root))
        def _():
            @pl.when(i <= SPLIT + depth0)
            def _():
                c_turn(0, i)

            @pl.when(i > SPLIT)
            def _():
                c_turn(1, i)

        @pl.when((i >= 4) & (i < 8))
        def _():
            weights(i - 4)

        for n, begin in enumerate(begins):
            first, count = groups[n]

            @pl.when((i >= begin) & (i < begin + blocks))
            def _():
                @pl.when(i == begin)
                def _():
                    build(first, count)

                block(first, count, i - begin, n == 0)

    first, count = groups[4]
    build(first, count)

    @pl.loop(0, blocks)
    def _(r):
        block(first, count, r, False)

    drain(0)
    drain(1)
    drain_rows()


def shards(pair_matrix, valence_index, conduction_index, valence_energy, conduction_energy):
    x = jnp.swapaxes(pair_matrix, 2, 3).reshape(96, 1024)
    return pl.pallas_call(
        kernel,
        out_shape=jax.ShapeDtypeStruct((2, 1024, 512), jnp.float32),
        in_specs=[pl.BlockSpec(memory_space=pltpu.HBM)] * 5,
        out_specs=pl.BlockSpec(memory_space=pltpu.VMEM),
        scratch_shapes=[
            pltpu.VMEM((96, 2, SUB, 512), jnp.bfloat16),
            pltpu.VMEM((96, SUB, 512), jnp.bfloat16),
            pltpu.VMEM((768, 1024), jnp.bfloat16),
            pltpu.VMEM((3, 512, 128), jnp.float32),
            pltpu.VMEM((3, 512), jnp.int32),
            pltpu.VMEM((3, 512), jnp.int32),
            pltpu.VMEM((16, 128), jnp.float32),
            pltpu.VMEM((16, 128), jnp.float32),
            pltpu.VMEM((2, 8, 512), jnp.int32),
            pltpu.SemaphoreType.DMA((5,)),
            pltpu.SemaphoreType.DMA((1,)),
            pltpu.SemaphoreType.DMA((2, LAST - 2)),
            pltpu.SemaphoreType.DMA((1,)),
            pltpu.SemaphoreType.DMA((5,)),
            pltpu.SemaphoreType.DMA((2, 4, 4)),
            pltpu.SemaphoreType.DMA((4, LAST + 1)),
        ],
        compiler_params=pltpu.CompilerParams(collective_id=0, has_side_effects=True, vmem_limit_bytes=40 << 20),
        cost_estimate=pl.CostEstimate(flops=6 << 30, bytes_accessed=4 << 20, transcendentals=0),
        name="chi",
    )(x, valence_index, conduction_index, valence_energy.reshape(16, 128), conduction_energy.reshape(16, 128))


def solution(mesh):
    in_specs = (P(None, None, "grow", "gcol"), P(), P(), P(), P())
    out_specs = P(None, "grow", "gcol")
    return jax.shard_map(shards, mesh=mesh, in_specs=in_specs, out_specs=out_specs, check_vma=False)
```

time: 383 us -> 75.8 us (0.20)
  the two profiles are of different devices: /device:TPU:1 before, /device:TPU:4 now
where the time goes in v2:
time: 75.8 us; the launch traced here: 75.5 us
  Pallas kernels  69.8 us (92%)
  local copies, waits for them, and re-layouts  5.73 us (8%)
    pallas_call x1, Pallas kernels, shards(): pl.pallas_call(kernel, out_shape=jax.ShapeDtypeStruct((2, 1024, 512), jnp...  69.8 us
    unnamed x11, local copies, waits for them, and re-layouts  5.73 us

profile of v2, /device:TPU:4, one launch (start us, length us, event | category | flops | bytes accessed | tf_op | source)
XLA Modules:
  0.0 75.5 jit_solution(2213601273342300840)
XLA Ops:
  0.0 0.0 copy-start
  0.0 0.9 %copy-done = bf16[3,2,1024,16]{2,3,1,0:T(8,128)(2,1)S(1)} copy-done((bf16[3,2,1024,16]{2,3,1,0:T(8,128)(2,1)S(1)}, bf16[3,2,1024,16]{2,3,1,0:T(8,128)(2,1)}, u32[]{:S(2)}) %copy-start) | copy-done | bytes 196632
  0.9 0.0 copy-start.1
  0.9 0.7 copy-done.1
  1.6 0.0 copy-start.2
  1.6 0.7 copy-done.2
  2.3 0.0 copy-start.3
  2.3 0.7 copy-done.3
  3.0 0.0 copy-start.4
  3.0 0.7 copy-done.4
  3.7 69.8 %chi.1 = f32[2,1024,512]{2,1,0:T(8,128)S(1)} custom-call(bf16[96,1024]{1,0:T(8,128)(2,1)S(1)} %bitcast.5, s32[3,512]{1,0:T(4,128)S(1)} %copy-done.1, s32[3,512]{1,0:T(4,128)S(1)} %copy-done.2, f32[16,128]{1,0:T(8,128)S(1)} %bitcast.6, f32[16,128]{1,0:T(8,128)S(1)} %bitcast.7), custom_call_target="tpu_custom_call" | custom-call | flops 6442450944 | bytes 4194304 | tf_op jit(solution)/shard_map/chi/pallas_call | solution.py:393
  73.5 2.0 %copy.7 = f32[2,1024,512]{2,1,0:T(8,128)} copy(f32[2,1024,512]{2,1,0:T(8,128)S(1)} %chi.1) | data formatting | bytes 8388608
Async XLA Ops:
  0.0 0.9 %copy-start = (bf16[3,2,1024,16]{2,3,1,0:T(8,128)(2,1)S(1)}, bf16[3,2,1024,16]{2,3,1,0:T(8,128)(2,1)}, u32[]{:S(2)}) copy-start(bf16[3,2,1024,16]{2,3,1,0:T(8,128)(2,1)} %param.5) | copy-start | bytes 589828
  0.9 0.7 copy-start.1
  1.6 0.7 copy-start.2
  2.3 0.7 copy-start.3
  3.0 0.7 copy-start.4

commit v3 on v2

--- a/solution.py
+++ b/solution.py
@@ -12,7 +12,7 @@
 DEEP = 16
 SUB = 32
 LAST = 26
-HOP = 2
+HOP = 3
 ROWS = 512
 
 TREES = [
@@ -27,7 +27,7 @@
         (0, 1): (1, 0), (0, 2): (3, 0), (2, 2): (1, 0),
     },
 ]
-SPLIT = 20
+SPLIT = 14
 STEPS = [(1, 0), (3, 0), (0, 1), (0, 3), (0, 2), (2, 0)]
 
 

time: 75.8 us -> 69.5 us (0.917)
  Pallas kernels: 69.8 us -> 63.4 us
    pallas_call x1, Pallas kernels: 69.8 us -> 63.4 us  [shards(): pl.pallas_call(kernel, out_shape=jax.ShapeDtypeStruct((2, 1024, 512), jnp...]
where the time goes in v3:
time: 69.5 us; the launch traced here: 69.2 us
  Pallas kernels  63.4 us (91%)
  local copies, waits for them, and re-layouts  5.73 us (8%)
    pallas_call x1, Pallas kernels, shards(): pl.pallas_call(kernel, out_shape=jax.ShapeDtypeStruct((2, 1024, 512), jnp...  63.4 us
    unnamed x11, local copies, waits for them, and re-layouts  5.73 us

profile of v3, /device:TPU:4, one launch (start us, length us, event | category | flops | bytes accessed | tf_op | source)
XLA Modules:
  0.0 69.2 jit_solution(3332429205552202177)
XLA Ops:
  0.0 0.0 copy-start
  0.0 0.9 %copy-done = bf16[3,2,1024,16]{2,3,1,0:T(8,128)(2,1)S(1)} copy-done((bf16[3,2,1024,16]{2,3,1,0:T(8,128)(2,1)S(1)}, bf16[3,2,1024,16]{2,3,1,0:T(8,128)(2,1)}, u32[]{:S(2)}) %copy-start) | copy-done | bytes 196632
  0.9 0.0 copy-start.1
  0.9 0.7 %copy-done.1 = s32[3,512]{1,0:T(4,128)S(1)} copy-done((s32[3,512]{1,0:T(4,128)S(1)}, s32[3,512]{1,0:T(4,128)}, u32[]{:S(2)}) %copy-start.1) | copy-done | bytes 6168
  1.6 0.0 copy-start.2
  1.6 0.7 %copy-done.2 = s32[3,512]{1,0:T(4,128)S(1)} copy-done((s32[3,512]{1,0:T(4,128)S(1)}, s32[3,512]{1,0:T(4,128)}, u32[]{:S(2)}) %copy-start.2) | copy-done | bytes 6168
  2.3 0.0 copy-start.3
  2.3 0.7 %copy-done.3 = f32[2048]{0:T(1024)S(1)} copy-done((f32[2048]{0:T(1024)S(1)}, f32[2048]{0:T(1024)}, u32[]{:S(2)}) %copy-start.3) | copy-done | bytes 8216
  3.0 0.0 copy-start.4
  3.0 0.7 %copy-done.4 = f32[2048]{0:T(1024)S(1)} copy-done((f32[2048]{0:T(1024)S(1)}, f32[2048]{0:T(1024)}, u32[]{:S(2)}) %copy-start.4) | copy-done | bytes 8216
  3.7 63.4 %chi.1 = f32[2,1024,512]{2,1,0:T(8,128)S(1)} custom-call(bf16[96,1024]{1,0:T(8,128)(2,1)S(1)} %bitcast.5, s32[3,512]{1,0:T(4,128)S(1)} %copy-done.1, s32[3,512]{1,0:T(4,128)S(1)} %copy-done.2, f32[16,128]{1,0:T(8,128)S(1)} %bitcast.6, f32[16,128]{1,0:T(8,128)S(1)} %bitcast.7), custom_call_target="tpu_custom_call" | custom-call | flops 6442450944 | bytes 4194304 | tf_op jit(solution)/shard_map/chi/pallas_call | solution.py:393
  67.1 2.0 %copy.7 = f32[2,1024,512]{2,1,0:T(8,128)} copy(f32[2,1024,512]{2,1,0:T(8,128)S(1)} %chi.1) | data formatting | bytes 8388608
Async XLA Ops:
  0.0 0.9 %copy-start = (bf16[3,2,1024,16]{2,3,1,0:T(8,128)(2,1)S(1)}, bf16[3,2,1024,16]{2,3,1,0:T(8,128)(2,1)}, u32[]{:S(2)}) copy-start(bf16[3,2,1024,16]{2,3,1,0:T(8,128)(2,1)} %param.5) | copy-start | bytes 589828
  0.9 0.7 %copy-start.1 = (s32[3,512]{1,0:T(4,128)S(1)}, s32[3,512]{1,0:T(4,128)}, u32[]{:S(2)}) copy-start(s32[3,512]{1,0:T(4,128)} %vi_hbm.1) | copy-start | bytes 18436
  1.6 0.7 %copy-start.2 = (s32[3,512]{1,0:T(4,128)S(1)}, s32[3,512]{1,0:T(4,128)}, u32[]{:S(2)}) copy-start(s32[3,512]{1,0:T(4,128)} %ci_hbm.1) | copy-start | bytes 18436
  2.3 0.7 %copy-start.3 = (f32[2048]{0:T(1024)S(1)}, f32[2048]{0:T(1024)}, u32[]{:S(2)}) copy-start(f32[2048]{0:T(1024)} %param.8) | copy-start | bytes 24580
  3.0 0.7 %copy-start.4 = (f32[2048]{0:T(1024)S(1)}, f32[2048]{0:T(1024)}, u32[]{:S(2)}) copy-start(f32[2048]{0:T(1024)} %param.9) | copy-start | bytes 24580

commit v4 on v3

--- a/solution.py
+++ b/solution.py
@@ -85,7 +85,7 @@
     return (sub == 2 * way) | ((sub == 1) & (core == way))
 
 
-def kernel(x_hbm, vi_hbm, ci_hbm, ve_hbm, ce_hbm, out_ref, rows_buf, cols_buf, rhs, wcol, vi_ref, ci_ref, ve_ref, ce_ref, ibuf,
+def kernel(x_hbm, index_hbm, energy_hbm, out_ref, rows_buf, cols_buf, rhs, wcol, index_ref, energy_ref, ibuf,
            isem, zsend, zrecv, dsend, drecv, csend, crecv):
     g = lax.axis_index("grow")
     gc = lax.axis_index("gcol")
@@ -95,7 +95,7 @@
 
     parts = [(x_hbm.at[SUB * k:SUB * (k + 1), 512 * h:512 * (h + 1)], rows_buf.at[3 * c + k, h])
              for k in range(3) for h in range(2)]
-    parts += [(vi_hbm, vi_ref), (ci_hbm, ci_ref), (ve_hbm, ve_ref), (ce_hbm, ce_ref)]
+    parts += [(index_hbm, index_ref), (energy_hbm, energy_ref)]
     loads = [pltpu.make_async_copy(src, dst, isem.at[max(n - 5, 0)]) for n, (src, dst) in enumerate(parts)]
     for load in loads:
         load.start()
@@ -265,11 +265,11 @@
     def weights(j):
         lanes = pl.ds(pl.multiple_of(j * 128, 128), 128)
 
-        def look(table, index):
+        def look(first, index):
             low, high = index & 127, index >> 7
             value = jnp.zeros((8, 128), jnp.float32)
             for r in range(16):
-                row = jnp.broadcast_to(table[r:r + 1, :], (8, 128))
+                row = jnp.broadcast_to(energy_ref[first + r:first + r + 1, :], (8, 128))
                 value = jnp.where(high == r, jnp.take_along_axis(row, low, axis=1), value)
             return value
 
@@ -278,10 +278,10 @@
             for load in loads[6:]:
                 load.wait()
             ibuf[...] = jnp.zeros_like(ibuf)
-            ibuf[0, 0:3, :] = vi_ref[...]
-            ibuf[1, 0:3, :] = ci_ref[...]
-
-        w = 2.0 / (look(ve_ref, ibuf[0, :, lanes]) - look(ce_ref, ibuf[1, :, lanes]))
+            ibuf[0, 0:3, :] = index_ref[0:3, :]
+            ibuf[1, 0:3, :] = index_ref[3:6, :]
+
+        w = 2.0 / (look(0, ibuf[0, :, lanes]) - look(16, ibuf[1, :, lanes]))
         for k in range(3):
             wcol[k, lanes, :] = jnp.broadcast_to(w[k:k + 1, :], (128, 128)).T
 
@@ -390,22 +390,22 @@
 
 def shards(pair_matrix, valence_index, conduction_index, valence_energy, conduction_energy):
     x = jnp.swapaxes(pair_matrix, 2, 3).reshape(96, 1024)
+    index = jnp.concatenate([valence_index, conduction_index])
+    energy = jnp.concatenate([valence_energy, conduction_energy]).reshape(32, 128)
     return pl.pallas_call(
         kernel,
         out_shape=jax.ShapeDtypeStruct((2, 1024, 512), jnp.float32),
-        in_specs=[pl.BlockSpec(memory_space=pltpu.HBM)] * 5,
+        in_specs=[pl.BlockSpec(memory_space=pltpu.HBM)] * 3,
         out_specs=pl.BlockSpec(memory_space=pltpu.VMEM),
         scratch_shapes=[
             pltpu.VMEM((96, 2, SUB, 512), jnp.bfloat16),
             pltpu.VMEM((96, SUB, 512), jnp.bfloat16),
             pltpu.VMEM((768, 1024), jnp.bfloat16),
             pltpu.VMEM((3, 512, 128), jnp.float32),
-            pltpu.VMEM((3, 512), jnp.int32),
-            pltpu.VMEM((3, 512), jnp.int32),
-            pltpu.VMEM((16, 128), jnp.float32),
-            pltpu.VMEM((16, 128), jnp.float32),
+            pltpu.VMEM((6, 512), jnp.int32),
+            pltpu.VMEM((32, 128), jnp.float32),
             pltpu.VMEM((2, 8, 512), jnp.int32),
-            pltpu.SemaphoreType.DMA((5,)),
+            pltpu.SemaphoreType.DMA((3,)),
             pltpu.SemaphoreType.DMA((1,)),
             pltpu.SemaphoreType.DMA((2, LAST - 2)),
             pltpu.SemaphoreType.DMA((1,)),
@@ -416,7 +416,7 @@
         compiler_params=pltpu.CompilerParams(collective_id=0, has_side_effects=True, vmem_limit_bytes=40 << 20),
         cost_estimate=pl.CostEstimate(flops=6 << 30, bytes_accessed=4 << 20, transcendentals=0),
         name="chi",
-    )(x, valence_index, conduction_index, valence_energy.reshape(16, 128), conduction_energy.reshape(16, 128))
+    )(x, index, energy)
 
 
 def solution(mesh):

time: 69.5 us -> 68.1 us (0.980)
  local copies, waits for them, and re-layouts: 5.73 us -> 2.94 us
  other arithmetic: 0 us -> 1.44 us
    unnamed x11 -> x3, local copies, waits for them, and re-layouts: 5.73 us -> 2.94 us
    concatenate x0 -> x2, other arithmetic: none -> 1.44 us  [the longest x1 0.72 us: shards(): index = jnp.concatenate([valence_index, conduction_index])]
where the time goes in v4:
time: 68.1 us; the launch traced here: 67.8 us
  Pallas kernels  63.4 us (93%)
  local copies, waits for them, and re-layouts  2.94 us (4%)
  other arithmetic  1.44 us (2%)
    pallas_call x1, Pallas kernels, shards(): pl.pallas_call(kernel, out_shape=jax.ShapeDtypeStruct((2, 1024, 512), jnp...  63.4 us
    unnamed x3, local copies, waits for them, and re-layouts  2.94 us

profile of v4, /device:TPU:4, one launch (start us, length us, event | category | flops | bytes accessed | tf_op | source)
XLA Modules:
  0.0 67.8 jit_solution(11745349072120892942)
XLA Ops:
  0.0 0.7 %pad_add_fusion.index_hbm = s32[6,512]{1,0:T(8,128)S(1)} fusion(s32[3,512]{1,0:T(4,128)} %param.7, s32[3,512]{1,0:T(4,128)} %param.6), kind=kLoop, calls=%fused_computation | loop fusion | flops 3072 | bytes 24576 | tf_op jit(solution)/shard_map/concatenate | solution.py:393
  0.7 0.7 %pad_maximum_fusion.energy_hbm = f32[32,128]{1,0:T(8,128)S(1)} fusion(f32[16,128]{1,0:T(8,128)} %bitcast.6, f32[16,128]{1,0:T(8,128)} %bitcast.7), kind=kLoop, calls=%fused_computation.1 | loop fusion | flops 4096 | bytes 32768 | tf_op jit(solution)/shard_map/concatenate | solution.py:394
  1.4 0.0 copy-start
  1.4 0.9 %copy-done = bf16[3,2,1024,16]{2,3,1,0:T(8,128)(2,1)S(1)} copy-done((bf16[3,2,1024,16]{2,3,1,0:T(8,128)(2,1)S(1)}, bf16[3,2,1024,16]{2,3,1,0:T(8,128)(2,1)}, u32[]{:S(2)}) %copy-start) | copy-done | bytes 196632
  2.4 63.4 %chi.1 = f32[2,1024,512]{2,1,0:T(8,128)S(1)} custom-call(bf16[96,1024]{1,0:T(8,128)(2,1)S(1)} %bitcast.5, s32[6,512]{1,0:T(8,128)S(1)} %pad_add_fusion.index_hbm, f32[32,128]{1,0:T(8,128)S(1)} %pad_maximum_fusion.energy_hbm), custom_call_target="tpu_custom_call" | custom-call | flops 6442450944 | bytes 4194304 | tf_op jit(solution)/shard_map/chi/pallas_call | solution.py:395
  65.8 2.0 %copy.7 = f32[2,1024,512]{2,1,0:T(8,128)} copy(f32[2,1024,512]{2,1,0:T(8,128)S(1)} %chi.1) | data formatting | bytes 8388608
Async XLA Ops:
  1.4 0.9 %copy-start = (bf16[3,2,1024,16]{2,3,1,0:T(8,128)(2,1)S(1)}, bf16[3,2,1024,16]{2,3,1,0:T(8,128)(2,1)}, u32[]{:S(2)}) copy-start(bf16[3,2,1024,16]{2,3,1,0:T(8,128)(2,1)} %param.5) | copy-start | bytes 589828

commit v5 on v4

--- a/solution.py
+++ b/solution.py
@@ -12,7 +12,7 @@
 DEEP = 16
 SUB = 32
 LAST = 26
-HOP = 3
+LAGS = [[0, 3, 6, 9, 12, 15], [0, 3, 6, 12]]
 ROWS = 512
 
 TREES = [
@@ -47,7 +47,6 @@
 NODES = [(px, py) for px in range(SIDE) for py in range(SIDE)]
 ROOT_FANS = [children_of(t, (0, 0)) for t in TREES]
 FAN = max(len(children_of(t, n)) for t in TREES for n in NODES if n != (0, 0))
-DEEPEST = [max(node_depth(t, n) for n in NODES) for t in TREES]
 
 
 def pick(place, values):
@@ -97,7 +96,7 @@
              for k in range(3) for h in range(2)]
     parts += [(index_hbm, index_ref), (energy_hbm, energy_ref)]
     loads = [pltpu.make_async_copy(src, dst, isem.at[max(n - 5, 0)]) for n, (src, dst) in enumerate(parts)]
-    for load in loads:
+    for load in loads[:6]:
         load.start()
 
     def grow_at(step):
@@ -114,15 +113,17 @@
     others += [dev(grow_at(s), z * 2 + k) for s in STEPS for k in range(2)]
     for other in others:
         pl.semaphore_signal(barrier, inc=1, device_id=other, device_id_type=MESH)
-
-    depths, fans, kids = [[], []], [[], []], [[], []]
+    for load in loads[6:]:
+        load.start()
+
+    lags, fans, kids = [[], []], [[], []], [[], []]
 
     def find_roles():
         px, py = dx, dy
         for tree in range(4):
             place = px * SIDE + py
             for kind, table in enumerate(TREES):
-                depths[kind].append(pick(place, [node_depth(table, n) for n in NODES]))
+                lags[kind].append(pick(place, [LAGS[kind][node_depth(table, n)] for n in NODES]))
                 lists = [children_of(table, n) if n != (0, 0) else [] for n in NODES]
                 fans[kind].append(pick(place, [len(v) for v in lists]))
                 mine = []
@@ -147,9 +148,9 @@
             send_sem=zsend.at[0], recv_sem=zrecv.at[way, i],
             device_id=dev(g, ends[way]), device_id_type=MESH)
 
-    def dcopy(slot):
+    def dcopy(slot, sub):
         return pltpu.make_async_remote_copy(
-            src_ref=rows_buf.at[pl.ds(3 * slot, 3)], dst_ref=rows_buf.at[pl.ds(3 * slot, 3)],
+            src_ref=rows_buf.at[3 * slot + sub], dst_ref=rows_buf.at[3 * slot + sub],
             send_sem=dsend.at[0], recv_sem=drecv.at[(slot + 2) >> 3],
             device_id=sibling, device_id_type=MESH)
 
@@ -204,18 +205,14 @@
                                 for copy in root_copies(kind, way, i):
                                     copy.start()
 
-        if not own:
-            @pl.when(sub == 2)
-            def _():
-                dcopy(slot_of(s, 0, c)).start()
-
-                @pl.when(s < 8)
-                def _():
-                    dcopy(slot_of(s, 1, c)).start()
+        for way in range(1 if own else 2):
+            @pl.when((s < 8) | far[way])
+            def _():
+                dcopy(slot_of(s, way, c), sub).start()
 
     def c_turn(kind, i):
         for tree in range(4):
-            j = i - HOP * depths[kind][tree]
+            j = i - lags[kind][tree]
             if kind == 0:
                 ok = (j >= 3 * (tree // 2)) & (j <= SPLIT)
             else:
@@ -329,7 +326,7 @@
 
     blocks = 1024 // ROWS
     groups = [(0, 6), (6, 8), (14, 8), (22, 8), (30, 2)]
-    depth0, depth1 = HOP * DEEPEST[0], HOP * DEEPEST[1]
+    depth0, depth1 = LAGS[0][-1], LAGS[1][-1]
 
     def ready(last_s):
         i = 3 * last_s + 2
@@ -338,12 +335,11 @@
     begins = [ready(s) for s in (1, 3, 5, 7)]
     turns = LAST + depth1 + 1
 
-    find_roles()
     arrival(rows_buf.at[pl.ds(3 * c, 3)], isem.at[0])
     pl.semaphore_wait(barrier, len(others))
     for i in range(3):
         z_turn(jnp.int32(i), own=True)
-    dcopy(c).start()
+    find_roles()
 
     @pl.loop(0, turns)
     def _(i):
@@ -376,6 +372,8 @@
 
                 block(first, count, i - begin, n == 0)
 
+    drain(0)
+    drain_rows()
     first, count = groups[4]
     build(first, count)
 
@@ -383,9 +381,7 @@
     def _(r):
         block(first, count, r, False)
 
-    drain(0)
     drain(1)
-    drain_rows()
 
 
 def shards(pair_matrix, valence_index, conduction_index, valence_energy, conduction_energy):

time: 68.1 us -> 67.8 us (level)
  no operation moved by 1% of the time
where the time goes in v5:
time: 67.8 us; the launch traced here: 67.5 us
  Pallas kernels  63.1 us (93%)
  local copies, waits for them, and re-layouts  2.94 us (4%)
  other arithmetic  1.44 us (2%)
    pallas_call x1, Pallas kernels, shards(): pl.pallas_call(kernel, out_shape=jax.ShapeDtypeStruct((2, 1024, 512), jnp...  63.1 us
    unnamed x3, local copies, waits for them, and re-layouts  2.94 us

profile of v5, /device:TPU:4, one launch (start us, length us, event | category | flops | bytes accessed | tf_op | source)
XLA Modules:
  0.0 67.5 jit_solution(1137216446461132594)
XLA Ops:
  0.0 0.7 %pad_add_fusion.index_hbm = s32[6,512]{1,0:T(8,128)S(1)} fusion(s32[3,512]{1,0:T(4,128)} %param.7, s32[3,512]{1,0:T(4,128)} %param.6), kind=kLoop, calls=%fused_computation | loop fusion | flops 3072 | bytes 24576 | tf_op jit(solution)/shard_map/concatenate | solution.py:389
  0.7 0.7 %pad_maximum_fusion.energy_hbm = f32[32,128]{1,0:T(8,128)S(1)} fusion(f32[16,128]{1,0:T(8,128)} %bitcast.6, f32[16,128]{1,0:T(8,128)} %bitcast.7), kind=kLoop, calls=%fused_computation.1 | loop fusion | flops 4096 | bytes 32768 | tf_op jit(solution)/shard_map/concatenate | solution.py:390
  1.4 0.0 copy-start
  1.4 0.9 %copy-done = bf16[3,2,1024,16]{2,3,1,0:T(8,128)(2,1)S(1)} copy-done((bf16[3,2,1024,16]{2,3,1,0:T(8,128)(2,1)S(1)}, bf16[3,2,1024,16]{2,3,1,0:T(8,128)(2,1)}, u32[]{:S(2)}) %copy-start) | copy-done | bytes 196632
  2.4 63.1 %chi.1 = f32[2,1024,512]{2,1,0:T(8,128)S(1)} custom-call(bf16[96,1024]{1,0:T(8,128)(2,1)S(1)} %bitcast.5, s32[6,512]{1,0:T(8,128)S(1)} %pad_add_fusion.index_hbm, f32[32,128]{1,0:T(8,128)S(1)} %pad_maximum_fusion.energy_hbm), custom_call_target="tpu_custom_call" | custom-call | flops 6442450944 | bytes 4194304 | tf_op jit(solution)/shard_map/chi/pallas_call | solution.py:391
  65.5 2.0 %copy.7 = f32[2,1024,512]{2,1,0:T(8,128)} copy(f32[2,1024,512]{2,1,0:T(8,128)S(1)} %chi.1) | data formatting | bytes 8388608
Async XLA Ops:
  1.4 0.9 %copy-start = (bf16[3,2,1024,16]{2,3,1,0:T(8,128)(2,1)S(1)}, bf16[3,2,1024,16]{2,3,1,0:T(8,128)(2,1)}, u32[]{:S(2)}) copy-start(bf16[3,2,1024,16]{2,3,1,0:T(8,128)(2,1)} %param.5) | copy-start | bytes 589828

commit v6 on v5

--- a/solution.py
+++ b/solution.py
@@ -84,7 +84,7 @@
     return (sub == 2 * way) | ((sub == 1) & (core == way))
 
 
-def kernel(x_hbm, index_hbm, energy_hbm, out_ref, rows_buf, cols_buf, rhs, wcol, index_ref, energy_ref, ibuf,
+def kernel(x_hbm, index_hbm, energy_hbm, out_ref, left_ref, rhs_ref, rows_buf, cols_buf, rhs, wcol, index_ref, energy_ref, ibuf,
            isem, zsend, zrecv, dsend, drecv, csend, crecv):
     g = lax.axis_index("grow")
     gc = lax.axis_index("gcol")
@@ -282,7 +282,7 @@
         for k in range(3):
             wcol[k, lanes, :] = jnp.broadcast_to(w[k:k + 1, :], (128, 128)).T
 
-    def build(first, count):
+    def build(first, count, rhs):
         def fill(load):
             @pl.loop(0, count)
             def _(n):
@@ -368,31 +368,45 @@
             def _():
                 @pl.when(i == begin)
                 def _():
-                    build(first, count)
+                    build(first, count, rhs)
 
                 block(first, count, i - begin, n == 0)
 
     drain(0)
     drain_rows()
     first, count = groups[4]
-    build(first, count)
-
-    @pl.loop(0, blocks)
-    def _(r):
-        block(first, count, r, False)
-
+    build(first, count, rhs_ref)
+    left_ref[...] = rows_buf[3 * first:3 * (first + count)]
     drain(1)
+
+
+def finish(sum_ref, left_ref, rhs_ref, out_ref, part_buf, osem):
+    def write(r):
+        at = pl.ds(pl.multiple_of(r * 256, 256), 256)
+        return pltpu.make_async_copy(part_buf.at[:, at], out_ref.at[:, at], osem.at[r])
+
+    for r in range(4):
+        left = left_ref[:, r // 2, :, (r % 2) * 256:(r % 2 + 1) * 256].reshape(6 * SUB, 256)
+        value = lax.dot_general(left, rhs_ref[...], (((0,), (0,)), ((), ())), preferred_element_type=jnp.float32)
+        for part in range(2):
+            at = slice(r * 256, (r + 1) * 256)
+            part_buf[part, at, :] = sum_ref[part, at, :] + value[:, part * 512:(part + 1) * 512]
+        write(r).start()
+    for r in range(4):
+        write(r).wait()
 
 
 def shards(pair_matrix, valence_index, conduction_index, valence_energy, conduction_energy):
     x = jnp.swapaxes(pair_matrix, 2, 3).reshape(96, 1024)
     index = jnp.concatenate([valence_index, conduction_index])
     energy = jnp.concatenate([valence_energy, conduction_energy]).reshape(32, 128)
-    return pl.pallas_call(
+    total, left, right = pl.pallas_call(
         kernel,
-        out_shape=jax.ShapeDtypeStruct((2, 1024, 512), jnp.float32),
+        out_shape=[jax.ShapeDtypeStruct((2, 1024, 512), jnp.float32),
+                   jax.ShapeDtypeStruct((6, 2, SUB, 512), jnp.bfloat16),
+                   jax.ShapeDtypeStruct((6 * SUB, 1024), jnp.bfloat16)],
         in_specs=[pl.BlockSpec(memory_space=pltpu.HBM)] * 3,
-        out_specs=pl.BlockSpec(memory_space=pltpu.VMEM),
+        out_specs=[pl.BlockSpec(memory_space=pltpu.VMEM)] * 3,
         scratch_shapes=[
             pltpu.VMEM((96, 2, SUB, 512), jnp.bfloat16),
             pltpu.VMEM((96, SUB, 512), jnp.bfloat16),
@@ -409,10 +423,19 @@
             pltpu.SemaphoreType.DMA((2, 4, 4)),
             pltpu.SemaphoreType.DMA((4, LAST + 1)),
         ],
-        compiler_params=pltpu.CompilerParams(collective_id=0, has_side_effects=True, vmem_limit_bytes=40 << 20),
+        compiler_params=pltpu.CompilerParams(collective_id=0, has_side_effects=True, vmem_limit_bytes=32 << 20),
         cost_estimate=pl.CostEstimate(flops=6 << 30, bytes_accessed=4 << 20, transcendentals=0),
         name="chi",
     )(x, index, energy)
+    return pl.pallas_call(
+        finish,
+        out_shape=jax.ShapeDtypeStruct((2, 1024, 512), jnp.float32),
+        in_specs=[pl.BlockSpec(memory_space=pltpu.VMEM)] * 3,
+        out_specs=pl.BlockSpec(memory_space=pl.ANY),
+        scratch_shapes=[pltpu.VMEM((2, 1024, 512), jnp.float32), pltpu.SemaphoreType.DMA((4,))],
+        compiler_params=pltpu.CompilerParams(vmem_limit_bytes=16 << 20),
+        name="finish",
+    )(total, left, right)
 
 
 def solution(mesh):

time: 67.8 us -> 67.3 us (level)
  local copies, waits for them, and re-layouts: 2.94 us -> 0.93 us
  Pallas kernels: 63.1 us -> 64.6 us
    unnamed x3 -> x2, local copies, waits for them, and re-layouts: 2.94 us -> 0.93 us
    pallas_call x1 -> x2, Pallas kernels: 63.1 us -> 64.6 us  [the longest x1 62.2 us: shards(): pl.pallas_call(kernel, out_shape=[jax.ShapeDtypeStruct((2, 1024, 512), jn...]
where the time goes in v6:
time: 67.3 us; the launch traced here: 66.9 us
  Pallas kernels  64.6 us (96%)
  other arithmetic  1.44 us (2%)
  local copies, waits for them, and re-layouts  0.93 us (1%)
    pallas_call x1, Pallas kernels, shards(): pl.pallas_call(kernel, out_shape=[jax.ShapeDtypeStruct((2, 1024, 512), jn...  62.2 us
    pallas_call x1, Pallas kernels, shards(): pl.pallas_call(finish, out_shape=jax.ShapeDtypeStruct((2, 1024, 512), jnp...  2.37 us

profile of v6, /device:TPU:4, one launch (start us, length us, event | category | flops | bytes accessed | tf_op | source)
XLA Modules:
  0.0 66.9 jit_solution(15918973519327921627)
XLA Ops:
  0.0 0.7 %pad_add_fusion.index_hbm = s32[6,512]{1,0:T(8,128)S(1)} fusion(s32[3,512]{1,0:T(4,128)} %param.7, s32[3,512]{1,0:T(4,128)} %param.6), kind=kLoop, calls=%fused_computation | loop fusion | flops 3072 | bytes 24576 | tf_op jit(solution)/shard_map/concatenate | solution.py:401
  0.7 0.7 %pad_maximum_fusion.energy_hbm = f32[32,128]{1,0:T(8,128)S(1)} fusion(f32[16,128]{1,0:T(8,128)} %bitcast.6, f32[16,128]{1,0:T(8,128)} %bitcast.7), kind=kLoop, calls=%fused_computation.1 | loop fusion | flops 4096 | bytes 32768 | tf_op jit(solution)/shard_map/concatenate | solution.py:402
  1.4 0.0 copy-start
  1.4 0.9 %copy-done = bf16[3,2,1024,16]{2,3,1,0:T(8,128)(2,1)S(1)} copy-done((bf16[3,2,1024,16]{2,3,1,0:T(8,128)(2,1)S(1)}, bf16[3,2,1024,16]{2,3,1,0:T(8,128)(2,1)}, u32[]{:S(2)}) %copy-start) | copy-done | bytes 196632
  2.4 62.2 %chi.1 = (f32[2,1024,512]{2,1,0:T(8,128)S(1)}, bf16[6,2,32,512]{3,2,1,0:T(8,128)(2,1)S(1)}, bf16[192,1024]{1,0:T(8,128)(2,1)S(1)}) custom-call(bf16[96,1024]{1,0:T(8,128)(2,1)S(1)} %bitcast.5, s32[6,512]{1,0:T(8,128)S(1)} %pad_add_fusion.index_hbm, f32[32,128]{1,0:T(8,128)S(1)} %pad_maximum_fusion.energy_hbm), custom_call_target="tpu_custom_call" | custom-call | flops 6442450944 | bytes 4194304 | tf_op jit(solution)/shard_map/chi/pallas_call | solution.py:403
  64.6 2.4 %finish.1 = f32[2,1024,512]{2,1,0:T(8,128)} custom-call(f32[2,1024,512]{2,1,0:T(8,128)S(1)} %get-tuple-element.8.sum_ref, bf16[6,2,32,512]{3,2,1,0:T(8,128)(2,1)S(1)} %get-tuple-element.9.left_ref, bf16[192,1024]{1,0:T(8,128)(2,1)S(1)} %get-tuple-element.10.rhs_ref), custom_call_target="tpu_custom_call" | custom-call | tf_op jit(solution)/shard_map/finish/pallas_call | solution.py:430
Async XLA Ops:
  1.4 0.9 %copy-start = (bf16[3,2,1024,16]{2,3,1,0:T(8,128)(2,1)S(1)}, bf16[3,2,1024,16]{2,3,1,0:T(8,128)(2,1)}, u32[]{:S(2)}) copy-start(bf16[3,2,1024,16]{2,3,1,0:T(8,128)(2,1)} %param.5) | copy-start | bytes 589828

commit v7 on v6

--- a/solution.py
+++ b/solution.py
@@ -12,7 +12,7 @@
 DEEP = 16
 SUB = 32
 LAST = 26
-LAGS = [[0, 3, 6, 9, 12, 15], [0, 3, 6, 12]]
+LAGS = [[0, 3, 6, 9, 12, 15], [0, 3, 6, 10]]
 ROWS = 512
 
 TREES = [

time: 67.3 us -> 67.3 us (level)
  no operation moved by 1% of the time
where the time goes in v7:
time: 67.3 us; the launch traced here: 66.9 us
  Pallas kernels  64.6 us (96%)
  other arithmetic  1.44 us (2%)
  local copies, waits for them, and re-layouts  0.93 us (1%)
    pallas_call x1, Pallas kernels, shards(): pl.pallas_call(kernel, out_shape=[jax.ShapeDtypeStruct((2, 1024, 512), jn...  62.2 us
    pallas_call x1, Pallas kernels, shards(): pl.pallas_call(finish, out_shape=jax.ShapeDtypeStruct((2, 1024, 512), jnp...  2.37 us

profile of v7, /device:TPU:4, one launch (start us, length us, event | category | flops | bytes accessed | tf_op | source)
XLA Modules:
  0.0 66.9 jit_solution(12106748535762382581)
XLA Ops:
  0.0 0.7 %pad_add_fusion.index_hbm = s32[6,512]{1,0:T(8,128)S(1)} fusion(s32[3,512]{1,0:T(4,128)} %param.7, s32[3,512]{1,0:T(4,128)} %param.6), kind=kLoop, calls=%fused_computation | loop fusion | flops 3072 | bytes 24576 | tf_op jit(solution)/shard_map/concatenate | solution.py:401
  0.7 0.7 %pad_maximum_fusion.energy_hbm = f32[32,128]{1,0:T(8,128)S(1)} fusion(f32[16,128]{1,0:T(8,128)} %bitcast.6, f32[16,128]{1,0:T(8,128)} %bitcast.7), kind=kLoop, calls=%fused_computation.1 | loop fusion | flops 4096 | bytes 32768 | tf_op jit(solution)/shard_map/concatenate | solution.py:402
  1.4 0.0 copy-start
  1.4 0.9 %copy-done = bf16[3,2,1024,16]{2,3,1,0:T(8,128)(2,1)S(1)} copy-done((bf16[3,2,1024,16]{2,3,1,0:T(8,128)(2,1)S(1)}, bf16[3,2,1024,16]{2,3,1,0:T(8,128)(2,1)}, u32[]{:S(2)}) %copy-start) | copy-done | bytes 196632
  2.4 62.2 %chi.1 = (f32[2,1024,512]{2,1,0:T(8,128)S(1)}, bf16[6,2,32,512]{3,2,1,0:T(8,128)(2,1)S(1)}, bf16[192,1024]{1,0:T(8,128)(2,1)S(1)}) custom-call(bf16[96,1024]{1,0:T(8,128)(2,1)S(1)} %bitcast.5, s32[6,512]{1,0:T(8,128)S(1)} %pad_add_fusion.index_hbm, f32[32,128]{1,0:T(8,128)S(1)} %pad_maximum_fusion.energy_hbm), custom_call_target="tpu_custom_call" | custom-call | flops 6442450944 | bytes 4194304 | tf_op jit(solution)/shard_map/chi/pallas_call | solution.py:403
  64.6 2.4 %finish.1 = f32[2,1024,512]{2,1,0:T(8,128)} custom-call(f32[2,1024,512]{2,1,0:T(8,128)S(1)} %get-tuple-element.8.sum_ref, bf16[6,2,32,512]{3,2,1,0:T(8,128)(2,1)S(1)} %get-tuple-element.9.left_ref, bf16[192,1024]{1,0:T(8,128)(2,1)S(1)} %get-tuple-element.10.rhs_ref), custom_call_target="tpu_custom_call" | custom-call | tf_op jit(solution)/shard_map/finish/pallas_call | solution.py:430
Async XLA Ops:
  1.4 0.9 %copy-start = (bf16[3,2,1024,16]{2,3,1,0:T(8,128)(2,1)S(1)}, bf16[3,2,1024,16]{2,3,1,0:T(8,128)(2,1)}, u32[]{:S(2)}) copy-start(bf16[3,2,1024,16]{2,3,1,0:T(8,128)(2,1)} %param.5) | copy-start | bytes 589828
